TPU v7x, 1024 devices: a whole 4x4x32 slice. The times are simulated.
1024 devices in a mesh: comp: 16 (over z_hi, y, core), row: 64 (over z_lo, x).
Axes of the slice: x: 4, y: 4, z: 32 (z_hi: 2, z_lo: 16; z = z_hi * 16 + z_lo), core: 2. Of those that a mesh axis runs over, the one named last changes fastest.
Arguments:
- fourier: bfloat16 [2, 1024, 49152], P(None, 'comp', 'row'), may hold values from -6 to 6
- legendre: bfloat16 [1024, 1024, 1024], P(('comp', 'row')), may hold values from -5 to 5
- gauss_weight: float32 [1024], replicated, may hold values from 0.5 to 2
- kappa_spec: bfloat16 [48], replicated, may hold values from 1 to 16
- marine_tracer_fields: float32 [2, 4, 256, 8192], P(None, None, 'comp', 'row'), may hold values from -6 to 6
- kappa_h: float32 [4, 256, 8192], P(None, 'comp', 'row'), may hold values from 0.04 to 0.18
- kappa_v: float32 [4], replicated, may hold values from 0.02 to 0.12
- air_flux: bfloat16 [2, 64, 8192], P(None, 'comp', 'row'), may hold values from -6 to 6
- remap_weight: bfloat16 [64, 64, 2, 128, 128], P('comp', 'row'), may hold values from -0.375 to 0.375
- remap_source: int32 [64, 64, 2], P('comp', 'row'), may hold values from 0 to 255
Outputs:
- smoothed_harmonic_coefficients: bfloat16 [2, 1024, 49152], P(None, 'comp', 'row')
- ocean_out: float32 [2, 4, 256, 8192], P(None, None, 'comp', 'row')
- seawater_heat_on_aerial_grid: float32 [64, 8192], P('comp', 'row')
Inputs may be any that keep to these rules, and one draw needn't show every extreme that they name: `remap_source`: entry (a, r, k) is the ocean row, within column band r, of the k-th source block of atmosphere block a.
All inputs are finite; a program needn't handle non-finite values.
Results may differ from a plain program's by a relative error of at most 0.0055.
Values may be sent and summed in bfloat16 or wider, within the bound.
A program may use at most 32 MiB of HBM per device.

v0:
```python
import jax
import jax.numpy as jnp
from jax import lax
from jax.sharding import PartitionSpec as P

NSTEP = 4


def padded_2(value, sides, width):
    for axis, dim in sides:
        size, length = (lax.axis_size(axis), value.shape[dim])
        up = [(i, (i + 1) % size) for i in range(size)]
        down = [(j, i) for i, j in up]
        last = lax.slice_in_dim(value, length - width, length, axis=dim)
        first = lax.slice_in_dim(value, 0, width, axis=dim)
        before = lax.ppermute(last, axis, up)
        after = lax.ppermute(first, axis, down)
        value = jnp.concatenate([before, value, after], axis=dim)
    return value


def spectral_filter(coeffs, degrees, kappa_wide, top_degree):
    ratio = degrees * (degrees + 1.0) / (top_degree * (top_degree + 1.0))
    factor = 1.0 / (1.0 + kappa_wide[None, :] * (ratio * ratio)[:, None])
    return (coeffs * factor).astype(jnp.bfloat16)


def spectral_columns(
    northern_raw, southern_raw, kappa_wide, gauss_weight, legendre_rows, wave, top_degree
):
    nhalf = legendre_rows.shape[0]
    columns = northern_raw.shape[1]
    northern = northern_raw.astype(jnp.float32)
    southern = southern_raw.astype(jnp.float32)
    weights = gauss_weight[:, None]
    even_part = (weights * (northern + southern)).astype(jnp.bfloat16)
    odd_part = (weights * (northern - southern)).astype(jnp.bfloat16)
    half_width = legendre_rows.shape[1] // 2
    both_parts = jnp.concatenate([even_part, odd_part], axis=1)
    dims = (((0,), (0,)), ((), ()))
    spectra = (
        lax.dot_general(legendre_rows, both_parts, dims, preferred_element_type=jnp.float32) / nhalf
    )
    even_spec = spectra[:half_width, :columns]
    odd_spec = spectra[half_width:, columns:]
    degrees = 2 * jnp.arange(half_width, dtype=jnp.int32) + wave
    even_filt = spectral_filter(even_spec, degrees.astype(jnp.float32), kappa_wide, top_degree)
    odd_filt = spectral_filter(odd_spec, (degrees + 1).astype(jnp.float32), kappa_wide, top_degree)
    upper = jnp.concatenate([even_filt, even_filt], axis=1)
    lower = jnp.concatenate([odd_filt, -odd_filt], axis=1)
    back_spec = jnp.concatenate([upper, lower], axis=0)
    grids = jnp.dot(legendre_rows, back_spec, preferred_element_type=jnp.float32)
    return jnp.stack([grids[:, :columns], grids[:, columns:]]).astype(jnp.bfloat16)


def advance(padded, kappa_cells, kappa_v, first_row, total_rows):
    centre = padded[:, :, 1:-1, 1:-1]
    upward = padded[:, :, :-2, 1:-1]
    downward = padded[:, :, 2:, 1:-1]
    western = padded[:, :, 1:-1, :-2]
    eastern = padded[:, :, 1:-1, 2:]
    height = centre.shape[2]
    row_ids = jnp.remainder(first_row + jnp.arange(height, dtype=jnp.int32), total_rows)
    open_up = (row_ids != 0).astype(jnp.float32)[:, None]
    open_down = (row_ids != total_rows - 1).astype(jnp.float32)[:, None]
    lateral = (
        (upward - centre) * open_up
        + (downward - centre) * open_down
        + (eastern - centre)
        + (western - centre)
    )
    above = jnp.concatenate([centre[:, :1], centre[:, :-1]], axis=1)
    beneath = jnp.concatenate([centre[:, 1:], centre[:, -1:]], axis=1)
    vertical = above + beneath - 2.0 * centre
    return centre + kappa_cells * lateral + kappa_v[:, None, None] * vertical


def body(
    fourier,
    legendre,
    gauss_weight,
    kappa_spec,
    marine_tracer_fields,
    kappa_h,
    kappa_v,
    air_flux,
    remap_weight,
    remap_source,
):
    row_count = lax.axis_size("row")
    comp_count = lax.axis_size("comp")
    nhalf = legendre.shape[1]
    legendre_rows = legendre[0]
    wave = lax.axis_index("comp") * row_count + lax.axis_index("row")
    top_degree = comp_count * row_count + legendre_rows.shape[1] - 1
    column_count = kappa_spec.shape[0]
    lat_local = fourier.shape[2] // column_count
    band_view = fourier.reshape(2, fourier.shape[1], lat_local, column_count)
    moved = lax.all_to_all(band_view, "row", split_axis=1, concat_axis=2, tiled=True)
    combined = spectral_columns(
        moved[0, 0],
        moved[1, 0],
        kappa_spec.astype(jnp.float32),
        gauss_weight,
        legendre_rows,
        wave,
        top_degree,
    )
    combined = combined.reshape(2, 1, nhalf, column_count)
    returned = lax.all_to_all(combined, "row", split_axis=2, concat_axis=1, tiled=True)
    smoothed_harmonic_coefficients = returned.reshape(fourier.shape)
    tile_rows = marine_tracer_fields.shape[2]
    tile_cells = marine_tracer_fields.shape[3]
    total_rows = tile_rows * comp_count
    first_row = lax.axis_index("comp") * tile_rows
    remap_block_weight = remap_weight[:, 0]
    sources = remap_source[:, 0]
    topmost_seawater_warmth = marine_tracer_fields[0, 0].astype(jnp.bfloat16)
    latitude_lines_each_strip = lax.all_gather(topmost_seawater_warmth, "comp", axis=0, tiled=True)
    picked_nonzeros = latitude_lines_each_strip[sources]
    seawater_heat_on_aerial_grid = jnp.einsum(
        "uqe,uqez->uz", picked_nonzeros, remap_block_weight, preferred_element_type=jnp.float32
    )
    flux_count = air_flux.shape[0]
    contrib = jnp.einsum(
        "fbx,bkox->bkfo", air_flux, remap_block_weight, preferred_element_type=jnp.float32
    )
    flat_contrib = contrib.reshape(-1, flux_count * tile_cells)
    flat_sources = sources.reshape(-1)
    span_rows = jnp.arange(tile_rows * lax.axis_size("comp"), dtype=jnp.int32)
    select = (span_rows[:, None] == flat_sources[None, :]).astype(jnp.float32)
    forcing = lax.psum_scatter(
        jnp.dot(
            select,
            flat_contrib,
            precision=lax.Precision.HIGHEST,
            preferred_element_type=jnp.float32,
        ).astype(jnp.bfloat16),
        "comp",
        scatter_dimension=0,
        tiled=True,
    ).astype(jnp.float32)
    forcing = jnp.transpose(forcing.reshape(tile_rows, flux_count, tile_cells), (1, 0, 2))
    climate_snapshot = marine_tracer_fields.at[:, 0].add(forcing)
    for section in range(NSTEP):
        padded = padded_2(climate_snapshot, (("comp", 2), ("row", 3)), 1)
        climate_snapshot = advance(padded, kappa_h, kappa_v, first_row, total_rows)
    return (smoothed_harmonic_coefficients, climate_snapshot, seawater_heat_on_aerial_grid)


def solution(mesh):
    return jax.shard_map(
        body,
        mesh=mesh,
        in_specs=(
            P(None, "comp", "row"),
            P(("comp", "row"), None, None),
            P(),
            P(),
            P(None, None, "comp", "row"),
            P(None, "comp", "row"),
            P(),
            P(None, "comp", "row"),
            P("comp", "row", None, None, None),
            P("comp", "row", None),
        ),
        out_specs=(P(None, "comp", "row"), P(None, None, "comp", "row"), P("comp", "row")),
        check_vma=False,
    )
```

profile of v0, /device:TPU:998, one launch (start us, length us, event | category | flops | bytes accessed | tf_op | source)
XLA Modules:
  0.0 420.7 jit_solution(9651098737984823686)
XLA Ops:
  7.2 1.0 copy.57
  8.2 1.5 reshape.182
  9.8 1.4 reshape.202
  11.2 22.8 %all-to-all-start = ((bf16[64,2,768]{2,1,0:T(2,128)(2,1)}), bf16[64,2,768]{2,1,0:T(2,128)(2,1)S(1)}, u32[]{:S(2)}, u32[]{:S(2)}) async-start(bf16[64,2,768]{2,1,0:T(2,128)(2,1)} %reshape.202), calls=%async_computation | async-start | bytes 393216 | tf_op jit(solution)/shard_map/all_to_all | solution.py:99
  34.0 0.0 reduce-scatter.2.cloned.1.call-start
  34.0 0.1 copy.32
  34.1 0.1 eq.21
  34.2 0.2 fusion.23
  34.4 0.9 convolution_convert_fusion
  35.3 0.0 reduce-scatter.2.cloned.1.call-update
  35.4 65.6 %all-gather = bf16[1,1,256,128]{3,2,1,0:T(8,128)(2,1)S(1)} all-gather(bf16[1,1,16,128]{3,2,1,0:T(8,128)(2,1)S(1)} %slice.321), channel_id=2, replica_groups=mesh['comp'=16,'row'=64] {'comp'}, dimensions={2}, use_global_device_ids=true | all-gather | bytes 69632 | tf_op jit(solution)/shard_map/all_gather | solution.py:119
  101.0 0.1 copy.35
  101.1 0.1 reshape.191
  101.2 0.6 gather_fusion
  101.7 0.7 fusion.21
  102.5 65.0 %reduce-scatter.2.cloned.1.call-done = bf16[16,256]{1,0:T(8,128)(2,1)} async-done(((bf16[256,256]{1,0:T(8,128)(2,1)}), bf16[16,256]{1,0:T(8,128)(2,1)}) %reduce-scatter.2.cloned.1.call-update) | async-done | bytes 8208 | tf_op jit(solution)/shard_map/reduce_scatter | solution.py:132
  167.5 0.7 constant_dynamic-update-slice_fusion
  168.2 5.1 %collective-permute-start.1 = (f32[2,4,1,128]{3,2,1,0:T(1,128)S(1)}, f32[2,4,1,128]{3,2,1,0:T(1,128)S(1)}, u32[]{:S(2)}, u32[]{:S(2)}) collective-permute-start(f32[2,4,1,128]{3,2,1,0:T(1,128)S(1)} %get-tuple-element.52), channel_id=1, source_target_pairs={{64,0},{128,64},{192,128},{256,192},{320,256},{384,320},{448,384},... | collective-permute-start | bytes 12296 | tf_op jit(solution)/shard_map/ppermute | solution.py:17
  173.3 1.9 collective-permute-start
  175.3 23.4 %collective-permute-done = f32[2,4,1,128]{3,2,1,0:T(1,128)S(1)} collective-permute-done((f32[2,4,1,128]{3,2,1,0:T(1,128)S(1)}, f32[2,4,1,128]{3,2,1,0:T(1,128)S(1)}, u32[]{:S(2)}, u32[]{:S(2)}) %collective-permute-start) | collective-permute-done | bytes 4128 | tf_op jit(solution)/shard_map/ppermute | solution.py:16
  198.7 0.1 fusion.109
  198.8 18.2 %collective-permute-start.3 = (f32[2,4,18,1]{3,2,1,0:T(8,128)S(1)}, f32[2,4,18,1]{3,2,1,0:T(8,128)S(1)}, u32[]{:S(2)}, u32[]{:S(2)}) collective-permute-start(f32[2,4,18,1]{3,2,1,0:T(8,128)S(1)} %get-tuple-element.30), channel_id=1, source_target_pairs={{0,1},{1,2},{2,3},{3,4},{4,5},{5,6},{6,7},{7,8},{8,9},{9,10},{10,1... | collective-permute-start | bytes 1736 | tf_op jit(solution)/shard_map/ppermute | solution.py:16
  217.0 1.9 collective-permute-start.2
  218.9 0.2 collective-permute-done.3
  219.2 22.6 %collective-permute-done.2 = f32[2,4,18,1]{3,2,1,0:T(8,128)S(1)} collective-permute-done((f32[2,4,18,1]{3,2,1,0:T(8,128)S(1)}, f32[2,4,18,1]{3,2,1,0:T(8,128)S(1)}, u32[]{:S(2)}, u32[]{:S(2)}) %collective-permute-start.2) | collective-permute-done | bytes 608 | tf_op jit(solution)/shard_map/ppermute | solution.py:17
  241.8 0.1 fusion.74
  242.0 1.9 collective-permute-start.5
  243.9 2.4 collective-permute-start.4
  246.4 22.9 %collective-permute-done.4 = f32[2,4,1,128]{3,2,1,0:T(1,128)S(1)} collective-permute-done((f32[2,4,1,128]{3,2,1,0:T(1,128)S(1)}, f32[2,4,1,128]{3,2,1,0:T(1,128)S(1)}, u32[]{:S(2)}, u32[]{:S(2)}) %collective-permute-start.4) | collective-permute-done | bytes 4128 | tf_op jit(solution)/shard_map/ppermute | solution.py:16
  269.3 0.1 fusion.108
  269.4 1.9 collective-permute-start.7
  271.3 3.9 collective-permute-start.6
  275.3 0.6 collective-permute-done.7
  275.9 20.3 %collective-permute-done.6 = f32[2,4,18,1]{3,2,1,0:T(8,128)S(1)} collective-permute-done((f32[2,4,18,1]{3,2,1,0:T(8,128)S(1)}, f32[2,4,18,1]{3,2,1,0:T(8,128)S(1)}, u32[]{:S(2)}, u32[]{:S(2)}) %collective-permute-start.6) | collective-permute-done | bytes 608 | tf_op jit(solution)/shard_map/ppermute | solution.py:17
  296.2 0.1 fusion.62
  296.3 1.9 collective-permute-start.9
  298.3 2.4 collective-permute-start.8
  300.7 23.0 %collective-permute-done.8 = f32[2,4,1,128]{3,2,1,0:T(1,128)S(1)} collective-permute-done((f32[2,4,1,128]{3,2,1,0:T(1,128)S(1)}, f32[2,4,1,128]{3,2,1,0:T(1,128)S(1)}, u32[]{:S(2)}, u32[]{:S(2)}) %collective-permute-start.8) | collective-permute-done | bytes 4128 | tf_op jit(solution)/shard_map/ppermute | solution.py:16
  323.7 0.1 fusion.107
  323.8 1.9 collective-permute-start.11
  325.8 3.9 collective-permute-start.10
  329.7 0.5 reshape.203
  330.2 0.1 convert_add_fusion
  330.3 0.2 fusion.17
  330.5 0.6 fusion.7
  331.2 0.1 fusion.104
  331.3 0.1 fusion.33
  331.4 0.8 fusion.13
  332.2 0.4 copy.30
  332.6 1.4 reshape.204
  334.0 22.8 %all-to-all-start.1 = ((bf16[64,2,768]{2,1,0:T(2,128)(2,1)}), bf16[64,2,768]{2,1,0:T(2,128)(2,1)S(1)}, u32[]{:S(2)}, u32[]{:S(2)}) async-start(bf16[64,2,768]{2,1,0:T(2,128)(2,1)} %reshape.204), calls=%async_computation.1 | async-start | bytes 393216 | tf_op jit(solution)/shard_map/all_to_all | solution.py:110
  356.8 0.1 fusion.50
  357.0 1.9 collective-permute-start.13
  358.9 2.4 collective-permute-start.12
  361.4 22.9 %collective-permute-done.12 = f32[2,4,1,128]{3,2,1,0:T(1,128)S(1)} collective-permute-done((f32[2,4,1,128]{3,2,1,0:T(1,128)S(1)}, f32[2,4,1,128]{3,2,1,0:T(1,128)S(1)}, u32[]{:S(2)}, u32[]{:S(2)}) %collective-permute-start.12) | collective-permute-done | bytes 4128 | tf_op jit(solution)/shard_map/ppermute | solution.py:16
  384.3 0.1 fusion.106
  384.4 2.1 collective-permute-start.15
  386.5 3.8 collective-permute-start.14
  390.3 0.6 collective-permute-done.15
  390.9 20.4 %collective-permute-done.14 = f32[2,4,18,1]{3,2,1,0:T(8,128)S(1)} collective-permute-done((f32[2,4,18,1]{3,2,1,0:T(8,128)S(1)}, f32[2,4,18,1]{3,2,1,0:T(8,128)S(1)}, u32[]{:S(2)}, u32[]{:S(2)}) %collective-permute-start.14) | collective-permute-done | bytes 608 | tf_op jit(solution)/shard_map/ppermute | solution.py:17
  411.3 0.8 fusion.38
  412.1 0.5 reshape.205
  412.6 0.1 copy.31
  412.7 1.2 reshape.183
  (49 shorter events, 0.3 us)
Async XLA Ops:
  7.2 323.4 %copy-start = (bf16[1,1024,1024]{2,1,0:T(8,128)(2,1)S(1)}, bf16[1,1024,1024]{2,1,0:T(8,128)(2,1)}, u32[]{:S(2)}) copy-start(bf16[1,1024,1024]{2,1,0:T(8,128)(2,1)} %param.13) | copy-start | bytes 6291460
  7.2 168.1 %copy-start.7 = (bf16[48]{0:T(256)(128)(2,1)S(1)}, bf16[48]{0:T(256)(128)(2,1)}, u32[]{:S(2)}) copy-start(bf16[48]{0:T(256)(128)(2,1)} %param.15) | copy-start | bytes 292
  7.2 27.0 %copy-start.6 = (bf16[2,4,128]{2,1,0:T(4,128)(2,1)S(1)}, bf16[2,4,128]{2,1,0:T(4,128)(2,1)}, u32[]{:S(2)}) copy-start(bf16[2,4,128]{2,1,0:T(4,128)(2,1)} %param.19) | copy-start | bytes 6148
  7.2 27.0 %copy-start.1 = (bf16[4,1,2,128,128]{4,3,2,1,0:T(8,128)(2,1)S(1)}, bf16[4,1,2,128,128]{4,3,2,1,0:T(8,128)(2,1)}, u32[]{:S(2)}) copy-start(bf16[4,1,2,128,128]{4,3,2,1,0:T(8,128)(2,1)} %param.20) | copy-start | bytes 786436
  7.2 26.8 %copy-start.5 = (s32[4,1,2]{0,2,1:T(2,128)S(1)}, s32[4,1,2]{0,2,1:T(2,128)}, u32[]{:S(2)}) copy-start(s32[4,1,2]{0,2,1:T(2,128)} %param.21) | copy-start | bytes 100
  9.8 232.1 %copy-start.2 = (f32[4,16,128]{2,1,0:T(8,128)S(1)}, f32[4,16,128]{2,1,0:T(8,128)}, u32[]{:S(2)}) copy-start(f32[4,16,128]{2,1,0:T(8,128)} %param.17) | copy-start | bytes 98308
  9.8 232.0 %copy-start.3 = (f32[4]{0:T(128)S(1)}, f32[4]{0:T(128)}, u32[]{:S(2)}) copy-start(f32[4]{0:T(128)} %param.18) | copy-start | bytes 52
  11.2 318.5 %all-to-all-start = ((bf16[64,2,768]{2,1,0:T(2,128)(2,1)}), bf16[64,2,768]{2,1,0:T(2,128)(2,1)S(1)}, u32[]{:S(2)}, u32[]{:S(2)}) async-start(bf16[64,2,768]{2,1,0:T(2,128)(2,1)} %reshape.202), calls=%async_computation | async-start | bytes 393216 | tf_op jit(solution)/shard_map/all_to_all | solution.py:99
  34.0 133.5 %reduce-scatter.2.cloned.1.call-start = ((), (), s32[]{:S(2)}) async-start(), calls=%async_computation.3 | async-start | bytes 139264 | tf_op jit(solution)/shard_map/reduce_scatter | solution.py:132
  168.2 7.1 %collective-permute-start.1 = (f32[2,4,1,128]{3,2,1,0:T(1,128)S(1)}, f32[2,4,1,128]{3,2,1,0:T(1,128)S(1)}, u32[]{:S(2)}, u32[]{:S(2)}) collective-permute-start(f32[2,4,1,128]{3,2,1,0:T(1,128)S(1)} %get-tuple-element.52), channel_id=1, source_target_pairs={{64,0},{128,64},{192,128},{256,192},{320,256},{384,320},{448,384},... | collective-permute-start | bytes 12296 | tf_op jit(solution)/shard_map/ppermute | solution.py:17
  173.3 25.4 %collective-permute-start = (f32[2,4,1,128]{3,2,1,0:T(1,128)S(1)}, f32[2,4,1,128]{3,2,1,0:T(1,128)S(1)}, u32[]{:S(2)}, u32[]{:S(2)}) collective-permute-start(f32[2,4,1,128]{3,2,1,0:T(1,128)S(1)} %get-tuple-element.51), channel_id=1, source_target_pairs={{0,64},{64,128},{128,192},{192,256},{256,320},{320,384},{384,448},... | collective-permute-start | bytes 12296 | tf_op jit(solution)/shard_map/ppermute | solution.py:16
  198.8 20.4 %collective-permute-start.3 = (f32[2,4,18,1]{3,2,1,0:T(8,128)S(1)}, f32[2,4,18,1]{3,2,1,0:T(8,128)S(1)}, u32[]{:S(2)}, u32[]{:S(2)}) collective-permute-start(f32[2,4,18,1]{3,2,1,0:T(8,128)S(1)} %get-tuple-element.30), channel_id=1, source_target_pairs={{0,1},{1,2},{2,3},{3,4},{4,5},{5,6},{6,7},{7,8},{8,9},{9,10},{10,1... | collective-permute-start | bytes 1736 | tf_op jit(solution)/shard_map/ppermute | solution.py:16
  217.0 24.8 %collective-permute-start.2 = (f32[2,4,18,1]{3,2,1,0:T(8,128)S(1)}, f32[2,4,18,1]{3,2,1,0:T(8,128)S(1)}, u32[]{:S(2)}, u32[]{:S(2)}) collective-permute-start(f32[2,4,18,1]{3,2,1,0:T(8,128)S(1)} %get-tuple-element.29), channel_id=1, source_target_pairs={{1,0},{2,1},{3,2},{4,3},{5,4},{6,5},{7,6},{8,7},{9,8},{10,9},{11,1... | collective-permute-start | bytes 1736 | tf_op jit(solution)/shard_map/ppermute | solution.py:17
  242.0 4.4 %collective-permute-start.5 = (f32[2,4,1,128]{3,2,1,0:T(1,128)S(1)}, f32[2,4,1,128]{3,2,1,0:T(1,128)S(1)}, u32[]{:S(2)}, u32[]{:S(2)}) collective-permute-start(f32[2,4,1,128]{3,2,1,0:T(1,128)S(1)} %get-tuple-element.48), channel_id=1, source_target_pairs={{64,0},{128,64},{192,128},{256,192},{320,256},{384,320},{448,384},... | collective-permute-start | bytes 12296 | tf_op jit(solution)/shard_map/ppermute | solution.py:17
  243.9 25.4 %collective-permute-start.4 = (f32[2,4,1,128]{3,2,1,0:T(1,128)S(1)}, f32[2,4,1,128]{3,2,1,0:T(1,128)S(1)}, u32[]{:S(2)}, u32[]{:S(2)}) collective-permute-start(f32[2,4,1,128]{3,2,1,0:T(1,128)S(1)} %get-tuple-element.47), channel_id=1, source_target_pairs={{0,64},{64,128},{128,192},{192,256},{256,320},{320,384},{384,448},... | collective-permute-start | bytes 12296 | tf_op jit(solution)/shard_map/ppermute | solution.py:16
  246.4 83.9 %copy-start.4 = (f32[1024]{0:T(1024)S(1)}, f32[1024]{0:T(1024)}, u32[]{:S(2)}) copy-start(f32[1024]{0:T(1024)} %param.14) | copy-start | bytes 12292
  269.4 6.5 %collective-permute-start.7 = (f32[2,4,18,1]{3,2,1,0:T(8,128)S(1)}, f32[2,4,18,1]{3,2,1,0:T(8,128)S(1)}, u32[]{:S(2)}, u32[]{:S(2)}) collective-permute-start(f32[2,4,18,1]{3,2,1,0:T(8,128)S(1)} %get-tuple-element.28), channel_id=1, source_target_pairs={{0,1},{1,2},{2,3},{3,4},{4,5},{5,6},{6,7},{7,8},{8,9},{9,10},{10,1... | collective-permute-start | bytes 1736 | tf_op jit(solution)/shard_map/ppermute | solution.py:16
  271.3 24.8 %collective-permute-start.6 = (f32[2,4,18,1]{3,2,1,0:T(8,128)S(1)}, f32[2,4,18,1]{3,2,1,0:T(8,128)S(1)}, u32[]{:S(2)}, u32[]{:S(2)}) collective-permute-start(f32[2,4,18,1]{3,2,1,0:T(8,128)S(1)} %get-tuple-element.27), channel_id=1, source_target_pairs={{1,0},{2,1},{3,2},{4,3},{5,4},{6,5},{7,6},{8,7},{9,8},{10,9},{11,1... | collective-permute-start | bytes 1736 | tf_op jit(solution)/shard_map/ppermute | solution.py:17
  296.3 4.4 %collective-permute-start.9 = (f32[2,4,1,128]{3,2,1,0:T(1,128)S(1)}, f32[2,4,1,128]{3,2,1,0:T(1,128)S(1)}, u32[]{:S(2)}, u32[]{:S(2)}) collective-permute-start(f32[2,4,1,128]{3,2,1,0:T(1,128)S(1)} %get-tuple-element.42), channel_id=1, source_target_pairs={{64,0},{128,64},{192,128},{256,192},{320,256},{384,320},{448,384},... | collective-permute-start | bytes 12296 | tf_op jit(solution)/shard_map/ppermute | solution.py:17
  298.3 25.5 %collective-permute-start.8 = (f32[2,4,1,128]{3,2,1,0:T(1,128)S(1)}, f32[2,4,1,128]{3,2,1,0:T(1,128)S(1)}, u32[]{:S(2)}, u32[]{:S(2)}) collective-permute-start(f32[2,4,1,128]{3,2,1,0:T(1,128)S(1)} %get-tuple-element.41), channel_id=1, source_target_pairs={{0,64},{64,128},{128,192},{192,256},{256,320},{320,384},{384,448},... | collective-permute-start | bytes 12296 | tf_op jit(solution)/shard_map/ppermute | solution.py:16
  323.8 33.0 %collective-permute-start.11 = (f32[2,4,18,1]{3,2,1,0:T(8,128)S(1)}, f32[2,4,18,1]{3,2,1,0:T(8,128)S(1)}, u32[]{:S(2)}, u32[]{:S(2)}) collective-permute-start(f32[2,4,18,1]{3,2,1,0:T(8,128)S(1)} %get-tuple-element.26), channel_id=1, source_target_pairs={{0,1},{1,2},{2,3},{3,4},{4,5},{5,6},{6,7},{7,8},{8,9},{9,10},{10,1... | collective-permute-start | bytes 1736 | tf_op jit(solution)/shard_map/ppermute | solution.py:16
  325.8 31.1 %collective-permute-start.10 = (f32[2,4,18,1]{3,2,1,0:T(8,128)S(1)}, f32[2,4,18,1]{3,2,1,0:T(8,128)S(1)}, u32[]{:S(2)}, u32[]{:S(2)}) collective-permute-start(f32[2,4,18,1]{3,2,1,0:T(8,128)S(1)} %get-tuple-element.25), channel_id=1, source_target_pairs={{1,0},{2,1},{3,2},{4,3},{5,4},{6,5},{7,6},{8,7},{9,8},{10,9},{11,1... | collective-permute-start | bytes 1736 | tf_op jit(solution)/shard_map/ppermute | solution.py:17
  334.0 78.1 %all-to-all-start.1 = ((bf16[64,2,768]{2,1,0:T(2,128)(2,1)}), bf16[64,2,768]{2,1,0:T(2,128)(2,1)S(1)}, u32[]{:S(2)}, u32[]{:S(2)}) async-start(bf16[64,2,768]{2,1,0:T(2,128)(2,1)} %reshape.204), calls=%async_computation.1 | async-start | bytes 393216 | tf_op jit(solution)/shard_map/all_to_all | solution.py:110
  357.0 4.4 %collective-permute-start.13 = (f32[2,4,1,128]{3,2,1,0:T(1,128)S(1)}, f32[2,4,1,128]{3,2,1,0:T(1,128)S(1)}, u32[]{:S(2)}, u32[]{:S(2)}) collective-permute-start(f32[2,4,1,128]{3,2,1,0:T(1,128)S(1)} %get-tuple-element.36), channel_id=1, source_target_pairs={{64,0},{128,64},{192,128},{256,192},{320,256},{384,320},{448,384},... | collective-permute-start | bytes 12296 | tf_op jit(solution)/shard_map/ppermute | solution.py:17
  358.9 25.4 %collective-permute-start.12 = (f32[2,4,1,128]{3,2,1,0:T(1,128)S(1)}, f32[2,4,1,128]{3,2,1,0:T(1,128)S(1)}, u32[]{:S(2)}, u32[]{:S(2)}) collective-permute-start(f32[2,4,1,128]{3,2,1,0:T(1,128)S(1)} %get-tuple-element.35), channel_id=1, source_target_pairs={{0,64},{64,128},{128,192},{192,256},{256,320},{320,384},{384,448},... | collective-permute-start | bytes 12296 | tf_op jit(solution)/shard_map/ppermute | solution.py:16
  384.4 6.5 %collective-permute-start.15 = (f32[2,4,18,1]{3,2,1,0:T(8,128)S(1)}, f32[2,4,18,1]{3,2,1,0:T(8,128)S(1)}, u32[]{:S(2)}, u32[]{:S(2)}) collective-permute-start(f32[2,4,18,1]{3,2,1,0:T(8,128)S(1)} %get-tuple-element.24), channel_id=1, source_target_pairs={{0,1},{1,2},{2,3},{3,4},{4,5},{5,6},{6,7},{7,8},{8,9},{9,10},{10,1... | collective-permute-start | bytes 1736 | tf_op jit(solution)/shard_map/ppermute | solution.py:16
  386.5 24.8 %collective-permute-start.14 = (f32[2,4,18,1]{3,2,1,0:T(8,128)S(1)}, f32[2,4,18,1]{3,2,1,0:T(8,128)S(1)}, u32[]{:S(2)}, u32[]{:S(2)}) collective-permute-start(f32[2,4,18,1]{3,2,1,0:T(8,128)S(1)} %get-tuple-element.23), channel_id=1, source_target_pairs={{1,0},{2,1},{3,2},{4,3},{5,4},{6,5},{7,6},{8,7},{9,8},{10,9},{11,1... | collective-permute-start | bytes 1736 | tf_op jit(solution)/shard_map/ppermute | solution.py:17
Sparse Core Ops, SparseCore 0:
  40.6 126.8 reduce-scatter.1
where the time goes:
time: 421 us
  waiting for transfers between devices  222 us (53%)
  starting transfers between devices  103 us (24%)
  blocking collectives  65.6 us (16%)
  between operations  14.6 us (3%)
  local copies, waits for them, and re-layouts  9.37 us (2%)
    ppermute x8, waiting for transfers between devices, padded_2(): before = lax.ppermute(last, axis, up)  93.7 us
    all_gather x1, blocking collectives, body(): lax.all_gather(topmost_seawater_warmth, 'comp', axis=0, tiled=True)  65.6 us
    reduce_scatter x1, waiting for transfers between devices, body(): lax.psum_scatter(jnp.dot(select, flat_contrib, precision=lax.Precision.HI...  65 us
    ppermute x8, waiting for transfers between devices, padded_2(): after = lax.ppermute(first, axis, down)  63.3 us
    ppermute x8, starting transfers between devices, padded_2(): before = lax.ppermute(last, axis, up)  33.2 us
    ppermute x8, starting transfers between devices, padded_2(): after = lax.ppermute(first, axis, down)  24.4 us
    all_to_all x1, starting transfers between devices, body(): lax.all_to_all(combined, 'row', split_axis=2, concat_axis=1, tiled=True)  22.8 us
    all_to_all x1, starting transfers between devices, body(): lax.all_to_all(band_view, 'row', split_axis=1, concat_axis=2, tiled=True)  22.8 us
  transfers between devices with their start and end apart: 19, of which 11 were waited for; matrix products, arithmetic and copies ran while one was open for 2% of the time, Pallas kernels for 0%

commit v1 on v0

v1 whole, which is shorter than its diff:
```python
import functools

import jax
import jax.numpy as jnp
from jax import lax
from jax.experimental import pallas as pl
from jax.experimental.pallas import tpu as pltpu
from jax.sharding import PartitionSpec as P

NSTEP = 4
MESH = pl.DeviceIdType.MESH
BF = jnp.bfloat16
F32 = jnp.float32
NN = (((1,), (0,)), ((), ()))
NT = (((1,), (1,)), ((), ()))
TN = (((0,), (0,)), ((), ()))


def dot(a, b, dims=NN):
    return lax.dot_general(a, b, dims, preferred_element_type=F32)


def iota(shape, axis):
    return lax.broadcasted_iota(jnp.int32, shape, axis)


def wait_bytes(ref, sem):
    pltpu.make_async_copy(ref, ref, sem).wait()


def kernel(
    four, leg_hbm, gauss, kappa, fields, kap_h, kap_v, flux, wts_hbm, srcs,
    out_spec, out_ocean, out_heat,
    leg, wts, perm_leg, send1, recv1, send2, gath, nspack, nsrecv, ewpack, ewrecv,
    loc_sem, send_sem, recv_sem,
):
    rows = lax.axis_size("row")
    comps = lax.axis_size("comp")
    me = lax.axis_index("row")
    comp = lax.axis_index("comp")
    half = comps // 2
    zhi = comp // half
    inner = lax.rem(comp, half)
    partner = lax.rem(comp + half, comps)
    north = lax.rem(comp + comps - 1, comps)
    south = lax.rem(comp + 1, comps)
    west = lax.rem(me + rows - 1, rows)
    east = lax.rem(me + 1, rows)

    load_leg = pltpu.make_async_copy(leg_hbm, leg, loc_sem.at[0])
    load_leg.start()
    load_wts = pltpu.make_async_copy(wts_hbm, wts, loc_sem.at[1])
    load_wts.start()

    barrier = pltpu.get_barrier_semaphore()

    def greet_row(k, _):
        target = lax.rem(me + k, rows)
        pl.semaphore_signal(barrier, inc=1, device_id={"row": target}, device_id_type=MESH)
        return 0

    def greet_comp(k, _):
        target = lax.rem(comp + k, comps)
        pl.semaphore_signal(barrier, inc=1, device_id={"comp": target}, device_id_type=MESH)
        return 0

    lax.fori_loop(1, rows, greet_row, 0)
    lax.fori_loop(1, comps, greet_comp, 0)

    wide = four.shape[2]
    cols = kappa.shape[1]
    lats = wide // cols
    mid = wide // 2
    lane_lat = iota((1, wide), 1) // cols
    weight = jnp.zeros((1, wide), F32)
    for l in range(lats):
        weight = jnp.where(lane_lat == l, gauss[me * lats + l], weight)
    n = four[0].astype(F32)
    s = four[1].astype(F32)
    even = (weight * (n + s)).astype(BF)
    odd = (weight * (n - s)).astype(BF)
    first = jnp.concatenate([even[:, :mid], odd[:, :mid]], axis=1)
    second = jnp.concatenate([even[:, mid:], odd[:, mid:]], axis=1)
    send1[:, 0, :] = first
    send1[:, 1, :] = second

    pl.semaphore_wait(barrier, rows + comps - 2)

    def send_forward(k, _):
        target = lax.rem(me + k, rows)
        pltpu.make_async_remote_copy(
            src_ref=send1.at[target], dst_ref=recv1.at[me], send_sem=send_sem.at[0], recv_sem=recv_sem.at[0],
            device_id={"row": target}, device_id_type=MESH).start()
        return 0

    lax.fori_loop(1, rows, send_forward, 0)
    own1 = pltpu.make_async_copy(send1.at[me], recv1.at[me], loc_sem.at[2])
    own1.start()

    load_wts.wait()
    tile = fields.shape[2]
    cells = fields.shape[3]
    blocks = wts.shape[0]
    kb = srcs.shape[0]
    row16 = iota((16, cells), 0)
    lane16 = iota((16, cells), 1)
    rep = jnp.zeros((16, cells), F32)
    for f in range(2):
        for j in range(blocks):
            rep = jnp.where(row16 == f * blocks + j, flux[f, j // kb, :].astype(F32)[None, :], rep)
    contrib = jnp.zeros((16, cells), F32)
    for j in range(blocks):
        only = jnp.where(lax.rem(row16, blocks) == j, rep, 0.0).astype(BF)
        contrib = contrib + dot(only, wts[j], NT)
    src_row = jnp.zeros((16, cells), F32)
    for j in range(blocks):
        hit = (lane16 // 16 == inner) & (lax.rem(lane16, blocks) == j) & (row16 == zhi)
        src_row = jnp.where(hit, srcs[j % kb, j // kb].astype(F32), src_row)
    gath[comp, 0:16, :] = fields[0, 0].astype(BF)
    gath[comp, 16:32, :] = contrib.astype(BF)
    gath[comp, 32:48, :] = src_row.astype(BF)
    across = pltpu.make_async_remote_copy(
        src_ref=gath.at[comp], dst_ref=gath.at[comp], send_sem=send_sem.at[1], recv_sem=recv_sem.at[1],
        device_id={"comp": partner}, device_id_type=MESH)
    across.start()

    def send_inner(slot, which):
        def step(k, _):
            target = zhi * half + lax.rem(inner + k, half)
            pltpu.make_async_remote_copy(
                src_ref=gath.at[slot], dst_ref=gath.at[slot], send_sem=send_sem.at[which], recv_sem=recv_sem.at[which],
                device_id={"comp": target}, device_id_type=MESH).start()
            return 0

        lax.fori_loop(1, half, step, 0)

    send_inner(comp, 2)

    slabs = [fields[t, k] for t in range(2) for k in range(4)] + [kap_h[k] for k in range(4)]
    count = len(slabs)
    row8 = iota((8, cells), 0)
    for p in range(count // 2):
        a, b = slabs[2 * p], slabs[2 * p + 1]
        nspack[0, p] = jnp.where(row8 < 4, a[:8], pltpu.roll(b[:8], 4, 0))
        nspack[1, p] = jnp.where(row8 >= 4, a[tile - 8 :], pltpu.roll(b[tile - 8 :], 4, 0))
    to_north = pltpu.make_async_remote_copy(
        src_ref=nspack.at[0], dst_ref=nsrecv.at[0], send_sem=send_sem.at[4], recv_sem=recv_sem.at[4],
        device_id={"comp": north}, device_id_type=MESH)
    to_south = pltpu.make_async_remote_copy(
        src_ref=nspack.at[1], dst_ref=nsrecv.at[1], send_sem=send_sem.at[5], recv_sem=recv_sem.at[5],
        device_id={"comp": south}, device_id_type=MESH)
    to_north.start()
    to_south.start()

    load_leg.wait()
    nlat = leg.shape[0]
    group = 2 * rows
    gi = iota((256, 256), 0)
    pick = (iota((256, 256), 1) == 8 * lax.rem(gi, 32) + gi // 32).astype(F32).astype(BF)
    for b in range(nlat // 256):
        part = dot(pick, leg[b * 256 : (b + 1) * 256, :]).astype(BF)
        for l in range(8):
            perm_leg[l * group + b * 32 : l * group + b * 32 + 32, :] = part[l * 32 : (l + 1) * 32, :]

    across.wait()
    send_inner(partner, 3)

    own1.wait()
    wait_bytes(recv1.at[pl.ds(0, rows - 1)], recv_sem.at[0])
    data = recv1[...].reshape(group, wide)
    hw = perm_leg.shape[1] // 2
    top = float((comps * rows + 2 * hw - 1) * (comps * rows + 2 * hw))
    wave = comp * rows + me
    grids = []
    for h in range(2):
        x = jnp.concatenate(
            [data[:, h * mid + l * cols : h * mid + (l + 1) * cols] for l in range(8)], axis=0
        )
        ph = perm_leg[:, h * hw : (h + 1) * hw]
        spec = dot(x, ph, TN) / nlat
        degree = (2 * iota((1, hw), 1) + wave + h).astype(F32)
        ratio = degree * (degree + 1.0) / top
        factor = 1.0 / (1.0 + kappa[...].T * (ratio * ratio))
        filt = (spec * factor).astype(BF)
        grids.append(dot(ph, filt, NT))
    upper = (grids[0] + grids[1]).astype(BF)
    lower = (grids[0] - grids[1]).astype(BF)
    back = jnp.concatenate(
        [g[l * group : (l + 1) * group, :] for g in (upper, lower) for l in range(8)], axis=1
    )
    send2[...] = back.reshape(rows, 2, wide)

    def send_back(k, _):
        target = lax.rem(me + k, rows)
        pltpu.make_async_remote_copy(
            src_ref=send2.at[target], dst_ref=out_spec.at[me], send_sem=send_sem.at[6], recv_sem=recv_sem.at[6],
            device_id={"row": target}, device_id_type=MESH).start()
        return 0

    lax.fori_loop(1, rows, send_back, 0)
    own2 = pltpu.make_async_copy(send2.at[me], out_spec.at[me], loc_sem.at[3])
    own2.start()

    wait_bytes(gath.at[pl.ds(0, half - 1)], recv_sem.at[2])
    wait_bytes(gath.at[pl.ds(0, half - 1)], recv_sem.at[3])
    total_rows = comps * tile
    held = tile + 8
    sst = gath[:, 0:16, :].reshape(total_rows, cells)
    contribs = gath[:, 16:32, :].reshape(comps * 16, cells)
    src16 = jnp.sum(gath[:, 32:48, :].astype(F32), axis=0).astype(jnp.int32)
    src = jnp.concatenate([src16[0:1, :], src16[1:2, :]], axis=1)
    pos = iota((2 * held, comps * 16), 0)
    pos_f = pos // held
    pos_y = pos - pos_f * held
    pos_y = jnp.where(pos_y < tile + 4, pos_y, pos_y - held)
    pos_y = lax.rem(comp * tile + pos_y + total_rows, total_rows)
    lane = iota((2 * held, comps * 16), 1)
    pick_f = (pos_y == src) & (lax.rem(lane // blocks, 2) == pos_f)
    forcing = dot(jnp.where(pick_f, 1.0, 0.0).astype(BF), contribs)

    to_north.wait()
    to_south.wait()
    wide_slabs = []
    for p in range(count // 2):
        from_south, from_north = nsrecv[0, p], nsrecv[1, p]
        halo_a = jnp.where(row8 < 4, from_south, from_north)
        halo_b = jnp.where(row8 < 4, pltpu.roll(from_south, 4, 0), pltpu.roll(from_north, 4, 0))
        wide_slabs.append(jnp.concatenate([slabs[2 * p], halo_a], axis=0))
        wide_slabs.append(jnp.concatenate([slabs[2 * p + 1], halo_b], axis=0))
    wide_slabs[0] = wide_slabs[0] + forcing[0:held]
    wide_slabs[4] = wide_slabs[4] + forcing[held:]

    lane24 = iota((held, cells), 1)
    westward = jnp.zeros((held, cells), F32)
    eastward = jnp.zeros((held, cells), F32)
    for i, slab in enumerate(wide_slabs):
        own_w = (lane24 >= 4 * i) & (lane24 < 4 * i + 4)
        own_e = (lane24 >= cells - 4 - 4 * i) & (lane24 < cells - 4 * i)
        westward = jnp.where(own_w, pltpu.roll(slab, 4 * i, 1), westward)
        eastward = jnp.where(own_e, pltpu.roll(slab, (cells - 4 * i) % cells, 1), eastward)
    ewpack[0] = westward
    ewpack[1] = eastward
    to_west = pltpu.make_async_remote_copy(
        src_ref=ewpack.at[0], dst_ref=ewrecv.at[0], send_sem=send_sem.at[7], recv_sem=recv_sem.at[7],
        device_id={"row": west}, device_id_type=MESH)
    to_east = pltpu.make_async_remote_copy(
        src_ref=ewpack.at[1], dst_ref=ewrecv.at[1], send_sem=send_sem.at[8], recv_sem=recv_sem.at[8],
        device_id={"row": east}, device_id_type=MESH)
    to_west.start()
    to_east.start()

    heat = jnp.zeros((8, cells), F32)
    prow = iota((8, total_rows), 0)
    plane = iota((8, total_rows), 1)
    hrow = iota((8, cells), 0)
    for k in range(kb):
        want = jnp.full((8, total_rows), -1, jnp.int32)
        for b in range(blocks // kb):
            want = jnp.where(prow == b, srcs[k, b], want)
        picked = dot(jnp.where(plane == want, 1.0, 0.0).astype(BF), sst).astype(BF)
        for b in range(blocks // kb):
            heat = heat + jnp.where(hrow == b, dot(picked, wts[b * kb + k]), 0.0)
    out_heat[...] = heat[0 : blocks // kb, :]

    to_west.wait()
    to_east.wait()
    from_east, from_west = ewrecv[0], ewrecv[1]
    sides = []
    for i in range(count):
        e_part = pltpu.roll(from_east, (cells - 4 * i) % cells, 1)
        w_part = pltpu.roll(from_west, 4 * i, 1)
        sides.append(jnp.where(lane24 < 4, e_part, jnp.where(lane24 >= cells - 4, w_part, 0.0)))
    ypos = iota((held, cells), 0)
    grow = comp * tile + jnp.where(ypos < tile + 4, ypos, ypos - held)
    grow = lax.rem(grow + total_rows, total_rows)
    up_open = (grow != 0).astype(F32)
    down_open = (grow != total_rows - 1).astype(F32)
    first_lane, last_lane = lane24 == 0, lane24 == cells - 1
    state = [(wide_slabs[i], sides[i]) for i in range(8)]
    kh = [(wide_slabs[8 + k], sides[8 + k]) for k in range(4)]
    for _ in range(NSTEP):
        new = []
        for t in range(2):
            for k in range(4):
                core, side = state[t * 4 + k]
                above = state[t * 4 + max(k - 1, 0)]
                below = state[t * 4 + min(k + 1, 3)]
                ce, se = pltpu.roll(core, cells - 1, 1), pltpu.roll(side, cells - 1, 1)
                cw, sw = pltpu.roll(core, 1, 1), pltpu.roll(side, 1, 1)
                easts = (jnp.where(last_lane, se, ce), jnp.where(last_lane, ce, se))
                wests = (jnp.where(first_lane, sw, cw), jnp.where(first_lane, cw, sw))
                pair = []
                for q in range(2):
                    v = state[t * 4 + k][q]
                    up = pltpu.roll(v, 1, 0)
                    down = pltpu.roll(v, held - 1, 0)
                    lateral = (up - v) * up_open + (down - v) * down_open + (easts[q] - v) + (wests[q] - v)
                    vertical = above[q] + below[q] - 2.0 * v
                    pair.append(v + kh[k][q] * lateral + kap_v[k] * vertical)
                new.append(tuple(pair))
        state = new
    for t in range(2):
        for k in range(4):
            out_ocean[t, k] = state[t * 4 + k][0][:tile]

    own2.wait()
    wait_bytes(send2.at[pl.ds(0, rows - 1)], recv_sem.at[6])
    wait_bytes(send1.at[pl.ds(0, rows - 1)], send_sem.at[0])
    wait_bytes(send2.at[pl.ds(0, rows - 1)], send_sem.at[6])
    wait_bytes(gath.at[pl.ds(0, half - 1)], send_sem.at[2])
    wait_bytes(gath.at[pl.ds(0, half - 1)], send_sem.at[3])


def body(
    fourier,
    legendre,
    gauss_weight,
    kappa_spec,
    marine_tracer_fields,
    kappa_h,
    kappa_v,
    air_flux,
    remap_weight,
    remap_source,
):
    rows = lax.axis_size("row")
    comps = lax.axis_size("comp")
    hemis, waves, wide = fourier.shape
    nlat, ns = legendre.shape[1:]
    tracers, levels, tile, cells = marine_tracer_fields.shape
    blocks = remap_weight.shape[0] * remap_weight.shape[2]
    vm = pl.BlockSpec(memory_space=pltpu.VMEM)
    sm = pl.BlockSpec(memory_space=pltpu.SMEM)
    anyspace = pl.BlockSpec(memory_space=pl.ANY)
    spectral, ocean, heat = pl.pallas_call(
        kernel,
        out_shape=(
            jax.ShapeDtypeStruct((waves, 2, wide), BF),
            jax.ShapeDtypeStruct(marine_tracer_fields.shape, F32),
            jax.ShapeDtypeStruct((remap_weight.shape[0], cells), F32),
        ),
        in_specs=[vm, anyspace, sm, vm, vm, vm, sm, vm, anyspace, sm],
        out_specs=(anyspace, vm, vm),
        scratch_shapes=[
            pltpu.VMEM((nlat, ns), BF),
            pltpu.VMEM((blocks, cells, cells), BF),
            pltpu.VMEM((nlat, ns), BF),
            pltpu.VMEM((waves, 2, wide), BF),
            pltpu.VMEM((waves, 2, wide), BF),
            pltpu.VMEM((waves, 2, wide), BF),
            pltpu.VMEM((comps, 48, cells), BF),
            pltpu.VMEM((2, 6, 8, cells), F32),
            pltpu.VMEM((2, 6, 8, cells), F32),
            pltpu.VMEM((2, tile + 8, cells), F32),
            pltpu.VMEM((2, tile + 8, cells), F32),
            pltpu.SemaphoreType.DMA((4,)),
            pltpu.SemaphoreType.DMA((9,)),
            pltpu.SemaphoreType.DMA((9,)),
        ],
        compiler_params=pltpu.CompilerParams(
            collective_id=0, has_side_effects=True, vmem_limit_bytes=48 * 2**20
        ),
    )(
        fourier,
        legendre[0],
        gauss_weight,
        kappa_spec.astype(F32).reshape(1, -1),
        marine_tracer_fields,
        kappa_h,
        kappa_v,
        air_flux,
        remap_weight.reshape(blocks, cells, cells),
        remap_source[:, 0, :].T,
    )
    spectral = spectral.reshape(waves, 2, hemis, wide // 2)
    spectral = jnp.transpose(spectral, (2, 0, 1, 3)).reshape(fourier.shape)
    return spectral, ocean, heat


def solution(mesh):
    return jax.shard_map(
        body,
        mesh=mesh,
        in_specs=(
            P(None, "comp", "row"),
            P(("comp", "row"), None, None),
            P(),
            P(),
            P(None, None, "comp", "row"),
            P(None, "comp", "row"),
            P(),
            P(None, "comp", "row"),
            P("comp", "row", None, None, None),
            P("comp", "row", None),
        ),
        out_specs=(P(None, "comp", "row"), P(None, None, "comp", "row"), P("comp", "row")),
        check_vma=False,
    )
```

time: 421 us -> 101 us (0.24)
  the two profiles are of different devices: /device:TPU:998 before, /device:TPU:24 now
where the time goes in v1:
time: 101 us; the launch traced here: 100 us
  Pallas kernels  89 us (88%)
  local copies, waits for them, and re-layouts  10.1 us (10%)
    pallas_call x1, Pallas kernels, body(): pl.pallas_call(kernel, out_shape=(jax.ShapeDtypeStruct((waves, 2, wide),...  89 us
    unnamed x20, local copies, waits for them, and re-layouts  8.97 us

profile of v1, /device:TPU:24, one launch (start us, length us, event | category | flops | bytes accessed | tf_op | source)
XLA Modules:
  0.0 100.4 jit_solution(7643948434207744038)
XLA Ops:
  0.6 0.7 bitcast_convert_fusion.kappa
  1.3 0.0 copy-start
  1.3 1.6 %copy-done = bf16[1,1024,1024]{2,1,0:T(8,128)(2,1)S(1)} copy-done((bf16[1,1024,1024]{2,1,0:T(8,128)(2,1)S(1)}, bf16[1,1024,1024]{2,1,0:T(8,128)(2,1)}, u32[]{:S(2)}) %copy-start) | copy-done | bytes 2097176
  2.9 0.0 copy-start.1
  2.9 0.9 copy-done.1
  3.8 0.0 copy-start.2
  3.8 0.9 copy-done.2
  4.8 0.0 copy-start.3
  4.8 0.8 copy-done.3
  5.6 0.0 copy-start.4
  5.6 0.8 copy-done.4
  6.4 0.0 copy-start.5
  6.4 0.7 copy-done.5
  7.0 0.0 copy-start.6
  7.0 0.7 copy-done.6
  7.7 0.0 copy-start.7
  7.7 0.7 copy-done.7
  8.4 0.0 copy-start.8
  8.4 0.7 copy-done.8
  9.1 89.0 %shard_map.121 = (bf16[64,2,768]{2,1,0:T(2,128)(2,1)S(1)}, f32[2,4,16,128]{3,2,1,0:T(8,128)S(1)}, f32[4,128]{1,0:T(4,128)S(1)}) custom-call(bf16[2,64,768]{2,1,0:T(8,128)(2,1)S(1)} %copy-done.2, bf16[1024,1024]{1,0:T(8,128)(2,1)S(1)} %bitcast.9, f32[1024]{0:T(1024)S(1)} %copy-done.5, f32[1,48]{1,0:T(1,128)S(1)} %bitcast_convert_fusion.kappa, ...), custom_call_target="tpu_custom_call" | custom-call | tf_op jit(solution)/shard_map/pallas_call | solution.py:335
  98.1 0.1 reshape.23
  98.2 0.2 copy.13
  98.4 0.8 reshape.24
  99.2 0.6 copy.16
  99.8 0.6 copy.17
Async XLA Ops:
  1.3 1.6 %copy-start = (bf16[1,1024,1024]{2,1,0:T(8,128)(2,1)S(1)}, bf16[1,1024,1024]{2,1,0:T(8,128)(2,1)}, u32[]{:S(2)}) copy-start(bf16[1,1024,1024]{2,1,0:T(8,128)(2,1)} %param.11) | copy-start | bytes 6291460
  2.9 0.9 copy-start.1
  3.8 0.9 copy-start.2
  4.8 0.8 copy-start.3
  5.6 0.8 copy-start.4
  6.4 0.7 copy-start.5
  7.0 0.7 copy-start.6
  7.7 0.7 copy-start.7
  8.4 0.7 copy-start.8

commit v2 on v1

--- a/solution.py
+++ b/solution.py
@@ -29,10 +29,11 @@
 
 
 def kernel(
-    four, leg_hbm, gauss, kappa, fields, kap_h, kap_v, flux, wts_hbm, srcs,
+    four_hbm, leg_hbm, gauss_hbm, kappa_hbm, fields_hbm, kap_h_hbm, kap_v_hbm, flux_hbm, wts_hbm, srcs_hbm,
     out_spec, out_ocean, out_heat,
-    leg, wts, perm_leg, send1, recv1, send2, gath, nspack, nsrecv, ewpack, ewrecv,
-    loc_sem, send_sem, recv_sem,
+    four, leg, gauss, kappa, fields, kap_h, kap_v, flux, wts, srcs,
+    perm_leg, send1, recv1, send2, gath, nspack, nsrecv, ewpack, ewrecv,
+    loc_sem, send_sem, recv_sem, ready, upper,
 ):
     rows = lax.axis_size("row")
     comps = lax.axis_size("comp")
@@ -47,31 +48,48 @@
     west = lax.rem(me + rows - 1, rows)
     east = lax.rem(me + 1, rows)
 
-    load_leg = pltpu.make_async_copy(leg_hbm, leg, loc_sem.at[0])
-    load_leg.start()
-    load_wts = pltpu.make_async_copy(wts_hbm, wts, loc_sem.at[1])
-    load_wts.start()
-
+    pairs = (
+        (four_hbm, four), (gauss_hbm, gauss), (flux_hbm, flux), (srcs_hbm, srcs), (fields_hbm, fields), (wts_hbm, wts),
+        (kap_h_hbm, kap_h), (kap_v_hbm, kap_v), (kappa_hbm, kappa), (leg_hbm, leg),
+    )
+    loads = [pltpu.make_async_copy(a, b, loc_sem.at[2 + i]) for i, (a, b) in enumerate(pairs)]
+    for load in loads:
+        load.start()
+
+    ahead = 1 - 2 * zhi
+    earlier = jnp.where(zhi == 0, me, rows - 1 - me)
+    later = rows - 1 - earlier
+    at_end = jnp.where((inner == 0) | (inner == half - 1), 1, 0)
+    across_end = jnp.where(inner == 0, north, south)
     barrier = pltpu.get_barrier_semaphore()
 
     def greet_row(k, _):
-        target = lax.rem(me + k, rows)
-        pl.semaphore_signal(barrier, inc=1, device_id={"row": target}, device_id_type=MESH)
+        pl.semaphore_signal(barrier, inc=1, device_id={"row": me + ahead * k}, device_id_type=MESH)
         return 0
 
     def greet_comp(k, _):
-        target = lax.rem(comp + k, comps)
+        target = zhi * half + lax.rem(inner + k, half)
         pl.semaphore_signal(barrier, inc=1, device_id={"comp": target}, device_id_type=MESH)
         return 0
 
-    lax.fori_loop(1, rows, greet_row, 0)
-    lax.fori_loop(1, comps, greet_comp, 0)
+    lax.fori_loop(1, later + 1, greet_row, 0)
+    lax.fori_loop(1, half, greet_comp, 0)
+
+    @pl.when(zhi == 0)
+    def _():
+        pl.semaphore_signal(barrier, inc=1, device_id={"comp": partner}, device_id_type=MESH)
+
+    @pl.when((zhi == 0) & (at_end == 1))
+    def _():
+        pl.semaphore_signal(barrier, inc=1, device_id={"comp": across_end}, device_id_type=MESH)
 
     wide = four.shape[2]
-    cols = kappa.shape[1]
+    cols = kappa.shape[0]
     lats = wide // cols
     mid = wide // 2
     lane_lat = iota((1, wide), 1) // cols
+    loads[0].wait()
+    loads[1].wait()
     weight = jnp.zeros((1, wide), F32)
     for l in range(lats):
         weight = jnp.where(lane_lat == l, gauss[me * lats + l], weight)
@@ -84,20 +102,37 @@
     send1[:, 0, :] = first
     send1[:, 1, :] = second
 
-    pl.semaphore_wait(barrier, rows + comps - 2)
-
-    def send_forward(k, _):
-        target = lax.rem(me + k, rows)
+    pl.semaphore_wait(barrier, earlier + half - 1 + zhi * (1 + at_end))
+
+    def answer_row(k, _):
+        pl.semaphore_signal(ready.at[me], inc=1, device_id={"row": me - ahead * k}, device_id_type=MESH)
+        return 0
+
+    lax.fori_loop(1, earlier + 1, answer_row, 0)
+
+    @pl.when(zhi == 1)
+    def _():
+        pl.semaphore_signal(upper, inc=1, device_id={"comp": partner}, device_id_type=MESH)
+
+    @pl.when((zhi == 1) & (at_end == 1))
+    def _():
+        pl.semaphore_signal(upper, inc=1, device_id={"comp": across_end}, device_id_type=MESH)
+
+    def forward_to(target):
         pltpu.make_async_remote_copy(
             src_ref=send1.at[target], dst_ref=recv1.at[me], send_sem=send_sem.at[0], recv_sem=recv_sem.at[0],
             device_id={"row": target}, device_id_type=MESH).start()
-        return 0
-
-    lax.fori_loop(1, rows, send_forward, 0)
-    own1 = pltpu.make_async_copy(send1.at[me], recv1.at[me], loc_sem.at[2])
+
+    def forward_earlier(k, _):
+        forward_to(me - ahead * (earlier + 1 - k))
+        return 0
+
+    lax.fori_loop(1, earlier + 1, forward_earlier, 0)
+    own1 = pltpu.make_async_copy(send1.at[me], recv1.at[me], loc_sem.at[0])
     own1.start()
 
-    load_wts.wait()
+    for load in loads[2:6]:
+        load.wait()
     tile = fields.shape[2]
     cells = fields.shape[3]
     blocks = wts.shape[0]
@@ -122,7 +157,10 @@
     across = pltpu.make_async_remote_copy(
         src_ref=gath.at[comp], dst_ref=gath.at[comp], send_sem=send_sem.at[1], recv_sem=recv_sem.at[1],
         device_id={"comp": partner}, device_id_type=MESH)
-    across.start()
+
+    @pl.when(zhi == 1)
+    def _():
+        across.start()
 
     def send_inner(slot, which):
         def step(k, _):
@@ -136,6 +174,7 @@
 
     send_inner(comp, 2)
 
+    loads[6].wait()
     slabs = [fields[t, k] for t in range(2) for k in range(4)] + [kap_h[k] for k in range(4)]
     count = len(slabs)
     row8 = iota((8, cells), 0)
@@ -149,10 +188,19 @@
     to_south = pltpu.make_async_remote_copy(
         src_ref=nspack.at[1], dst_ref=nsrecv.at[1], send_sem=send_sem.at[5], recv_sem=recv_sem.at[5],
         device_id={"comp": south}, device_id_type=MESH)
-    to_north.start()
-    to_south.start()
-
-    load_leg.wait()
+    north_first = (zhi == 1) | (inner > 0)
+    south_first = (zhi == 1) | (inner < half - 1)
+
+    @pl.when(north_first)
+    def _():
+        to_north.start()
+
+    @pl.when(south_first)
+    def _():
+        to_south.start()
+
+    for load in loads[7:]:
+        load.wait()
     nlat = leg.shape[0]
     group = 2 * rows
     gi = iota((256, 256), 0)
@@ -162,8 +210,13 @@
         for l in range(8):
             perm_leg[l * group + b * 32 : l * group + b * 32 + 32, :] = part[l * 32 : (l + 1) * 32, :]
 
-    across.wait()
-    send_inner(partner, 3)
+    def forward_later(k, _):
+        target = me + ahead * k
+        pl.semaphore_wait(ready.at[target], 1)
+        forward_to(target)
+        return 0
+
+    lax.fori_loop(1, later + 1, forward_later, 0)
 
     own1.wait()
     wait_bytes(recv1.at[pl.ds(0, rows - 1)], recv_sem.at[0])
@@ -171,6 +224,7 @@
     hw = perm_leg.shape[1] // 2
     top = float((comps * rows + 2 * hw - 1) * (comps * rows + 2 * hw))
     wave = comp * rows + me
+    kappa_col = kappa[...].astype(F32).reshape(1, cols).T
     grids = []
     for h in range(2):
         x = jnp.concatenate(
@@ -180,26 +234,44 @@
         spec = dot(x, ph, TN) / nlat
         degree = (2 * iota((1, hw), 1) + wave + h).astype(F32)
         ratio = degree * (degree + 1.0) / top
-        factor = 1.0 / (1.0 + kappa[...].T * (ratio * ratio))
+        factor = 1.0 / (1.0 + kappa_col * (ratio * ratio))
         filt = (spec * factor).astype(BF)
         grids.append(dot(ph, filt, NT))
-    upper = (grids[0] + grids[1]).astype(BF)
-    lower = (grids[0] - grids[1]).astype(BF)
+    north_grid = (grids[0] + grids[1]).astype(BF)
+    south_grid = (grids[0] - grids[1]).astype(BF)
     back = jnp.concatenate(
-        [g[l * group : (l + 1) * group, :] for g in (upper, lower) for l in range(8)], axis=1
+        [g[l * group : (l + 1) * group, :] for g in (north_grid, south_grid) for l in range(8)], axis=1
     )
     send2[...] = back.reshape(rows, 2, wide)
 
     def send_back(k, _):
-        target = lax.rem(me + k, rows)
+        step = (k + 1) // 2
+        turn = jnp.where(lax.rem(k, 2) == 1, step, rows - step)
+        target = lax.rem(me + turn, rows)
         pltpu.make_async_remote_copy(
             src_ref=send2.at[target], dst_ref=out_spec.at[me], send_sem=send_sem.at[6], recv_sem=recv_sem.at[6],
             device_id={"row": target}, device_id_type=MESH).start()
         return 0
 
     lax.fori_loop(1, rows, send_back, 0)
-    own2 = pltpu.make_async_copy(send2.at[me], out_spec.at[me], loc_sem.at[3])
+    own2 = pltpu.make_async_copy(send2.at[me], out_spec.at[me], loc_sem.at[1])
     own2.start()
+
+    @pl.when(zhi == 0)
+    def _():
+        pl.semaphore_wait(upper, 1 + at_end)
+        across.start()
+
+    @pl.when(jnp.logical_not(north_first))
+    def _():
+        to_north.start()
+
+    @pl.when(jnp.logical_not(south_first))
+    def _():
+        to_south.start()
+
+    across.wait_recv()
+    send_inner(partner, 3)
 
     wait_bytes(gath.at[pl.ds(0, half - 1)], recv_sem.at[2])
     wait_bytes(gath.at[pl.ds(0, half - 1)], recv_sem.at[3])
@@ -304,6 +376,7 @@
             out_ocean[t, k] = state[t * 4 + k][0][:tile]
 
     own2.wait()
+    across.wait_send()
     wait_bytes(send2.at[pl.ds(0, rows - 1)], recv_sem.at[6])
     wait_bytes(send1.at[pl.ds(0, rows - 1)], send_sem.at[0])
     wait_bytes(send2.at[pl.ds(0, rows - 1)], send_sem.at[6])
@@ -330,7 +403,6 @@
     tracers, levels, tile, cells = marine_tracer_fields.shape
     blocks = remap_weight.shape[0] * remap_weight.shape[2]
     vm = pl.BlockSpec(memory_space=pltpu.VMEM)
-    sm = pl.BlockSpec(memory_space=pltpu.SMEM)
     anyspace = pl.BlockSpec(memory_space=pl.ANY)
     spectral, ocean, heat = pl.pallas_call(
         kernel,
@@ -339,11 +411,19 @@
             jax.ShapeDtypeStruct(marine_tracer_fields.shape, F32),
             jax.ShapeDtypeStruct((remap_weight.shape[0], cells), F32),
         ),
-        in_specs=[vm, anyspace, sm, vm, vm, vm, sm, vm, anyspace, sm],
+        in_specs=[anyspace] * 10,
         out_specs=(anyspace, vm, vm),
         scratch_shapes=[
+            pltpu.VMEM(fourier.shape, BF),
             pltpu.VMEM((nlat, ns), BF),
+            pltpu.SMEM(gauss_weight.shape, F32),
+            pltpu.VMEM(kappa_spec.shape, BF),
+            pltpu.VMEM(marine_tracer_fields.shape, F32),
+            pltpu.VMEM(kappa_h.shape, F32),
+            pltpu.SMEM(kappa_v.shape, F32),
+            pltpu.VMEM(air_flux.shape, BF),
             pltpu.VMEM((blocks, cells, cells), BF),
+            pltpu.SMEM(remap_source.shape[:1:-1] + remap_source.shape[:1], jnp.int32),
             pltpu.VMEM((nlat, ns), BF),
             pltpu.VMEM((waves, 2, wide), BF),
             pltpu.VMEM((waves, 2, wide), BF),
@@ -353,18 +433,20 @@
             pltpu.VMEM((2, 6, 8, cells), F32),
             pltpu.VMEM((2, tile + 8, cells), F32),
             pltpu.VMEM((2, tile + 8, cells), F32),
-            pltpu.SemaphoreType.DMA((4,)),
+            pltpu.SemaphoreType.DMA((12,)),
             pltpu.SemaphoreType.DMA((9,)),
             pltpu.SemaphoreType.DMA((9,)),
+            pltpu.SemaphoreType.REGULAR((rows,)),
+            pltpu.SemaphoreType.REGULAR,
         ],
         compiler_params=pltpu.CompilerParams(
-            collective_id=0, has_side_effects=True, vmem_limit_bytes=48 * 2**20
+            collective_id=0, has_side_effects=True, vmem_limit_bytes=60 * 2**20
         ),
     )(
         fourier,
         legendre[0],
         gauss_weight,
-        kappa_spec.astype(F32).reshape(1, -1),
+        kappa_spec,
         marine_tracer_fields,
         kappa_h,
         kappa_v,

time: 101 us -> 82.2 us (0.81)
  the two profiles are of different devices: /device:TPU:24 before, /device:TPU:1 now
where the time goes in v2:
time: 82.2 us; the launch traced here: 81.2 us
  Pallas kernels  75.8 us (92%)
  local copies, waits for them, and re-layouts  4.73 us (6%)
    pallas_call x1, Pallas kernels, body(): pl.pallas_call(kernel, out_shape=(jax.ShapeDtypeStruct((waves, 2, wide),...  75.8 us
    unnamed x2, local copies, waits for them, and re-layouts  2.72 us

profile of v2, /device:TPU:1, one launch (start us, length us, event | category | flops | bytes accessed | tf_op | source)
XLA Modules:
  0.0 81.2 jit_solution(8304692411223603938)
XLA Ops:
  0.6 75.8 %shard_map.121 = (bf16[64,2,768]{2,1,0:T(2,128)(2,1)}, f32[2,4,16,128]{3,2,1,0:T(8,128)}, f32[4,128]{1,0:T(4,128)}) custom-call(bf16[2,64,768]{2,1,0:T(8,128)(2,1)} %four_hbm.1, bf16[1024,1024]{1,0:T(8,128)(2,1)} %bitcast.6, f32[1024]{0:T(1024)} %gauss_hbm.1, bf16[48]{0:T(256)(128)(2,1)} %kappa_hbm.1, f32[2,4,16,128]{3,2,1,0:T(8,128)} %fields_hbm.1, ...), custom_call_target="tpu_custom_call" | custom-call | tf_op jit(solution)/shard_map/pallas_call | solution.py:407
  76.4 1.1 %reshape.16 = bf16[64,2,2,384]{3,2,1,0:T(2,128)(2,1)S(1)} reshape(bf16[64,2,768]{2,1,0:T(2,128)(2,1)} %get-tuple-element.6) | data formatting | bytes 393216 | tf_op jit(solution)/shard_map/reshape | solution.py:457
  77.5 0.2 copy.13
  77.6 0.8 reshape.17
  78.4 1.5 %copy.16 = f32[2,4,16,128]{3,2,1,0:T(8,128)} copy(f32[2,4,16,128]{3,2,1,0:T(8,128)} %get-tuple-element.13) | data formatting | bytes 131072
  79.9 1.2 %copy.17 = f32[4,128]{1,0:T(4,128)} copy(f32[4,128]{1,0:T(4,128)} %get-tuple-element.14) | data formatting | bytes 4096

commit v3 on v2

--- a/solution.py
+++ b/solution.py
@@ -244,6 +244,22 @@
     )
     send2[...] = back.reshape(rows, 2, wide)
 
+    @pl.when(zhi == 0)
+    def _():
+        pl.semaphore_wait(upper, 1 + at_end)
+        across.start()
+
+    @pl.when(jnp.logical_not(north_first))
+    def _():
+        to_north.start()
+
+    @pl.when(jnp.logical_not(south_first))
+    def _():
+        to_south.start()
+
+    across.wait_recv()
+    send_inner(partner, 3)
+
     def send_back(k, _):
         step = (k + 1) // 2
         turn = jnp.where(lax.rem(k, 2) == 1, step, rows - step)
@@ -253,25 +269,9 @@
             device_id={"row": target}, device_id_type=MESH).start()
         return 0
 
-    lax.fori_loop(1, rows, send_back, 0)
+    lax.fori_loop(1, rows // 2 + 1, send_back, 0)
     own2 = pltpu.make_async_copy(send2.at[me], out_spec.at[me], loc_sem.at[1])
     own2.start()
-
-    @pl.when(zhi == 0)
-    def _():
-        pl.semaphore_wait(upper, 1 + at_end)
-        across.start()
-
-    @pl.when(jnp.logical_not(north_first))
-    def _():
-        to_north.start()
-
-    @pl.when(jnp.logical_not(south_first))
-    def _():
-        to_south.start()
-
-    across.wait_recv()
-    send_inner(partner, 3)
 
     wait_bytes(gath.at[pl.ds(0, half - 1)], recv_sem.at[2])
     wait_bytes(gath.at[pl.ds(0, half - 1)], recv_sem.at[3])
@@ -320,6 +320,8 @@
         device_id={"row": east}, device_id_type=MESH)
     to_west.start()
     to_east.start()
+
+    lax.fori_loop(rows // 2 + 1, rows, send_back, 0)
 
     heat = jnp.zeros((8, cells), F32)
     prow = iota((8, total_rows), 0)

time: 82.2 us -> 74.7 us (0.909)
  Pallas kernels: 75.8 us -> 69 us
    pallas_call x1, Pallas kernels: 75.8 us -> 69 us  [body(): pl.pallas_call(kernel, out_shape=(jax.ShapeDtypeStruct((waves, 2, wide),...]
where the time goes in v3:
time: 74.7 us; the launch traced here: 74.4 us
  Pallas kernels  69 us (92%)
  local copies, waits for them, and re-layouts  4.73 us (6%)
    pallas_call x1, Pallas kernels, body(): pl.pallas_call(kernel, out_shape=(jax.ShapeDtypeStruct((waves, 2, wide),...  69 us
    unnamed x2, local copies, waits for them, and re-layouts  2.72 us

profile of v3, /device:TPU:1, one launch (start us, length us, event | category | flops | bytes accessed | tf_op | source)
XLA Modules:
  0.0 74.4 jit_solution(2792114016172023080)
XLA Ops:
  0.6 69.0 %shard_map.121 = (bf16[64,2,768]{2,1,0:T(2,128)(2,1)}, f32[2,4,16,128]{3,2,1,0:T(8,128)}, f32[4,128]{1,0:T(4,128)}) custom-call(bf16[2,64,768]{2,1,0:T(8,128)(2,1)} %four_hbm.1, bf16[1024,1024]{1,0:T(8,128)(2,1)} %bitcast.6, f32[1024]{0:T(1024)} %gauss_hbm.1, bf16[48]{0:T(256)(128)(2,1)} %kappa_hbm.1, f32[2,4,16,128]{3,2,1,0:T(8,128)} %fields_hbm.1, ...), custom_call_target="tpu_custom_call" | custom-call | tf_op jit(solution)/shard_map/pallas_call | solution.py:409
  69.7 1.1 %reshape.16 = bf16[64,2,2,384]{3,2,1,0:T(2,128)(2,1)S(1)} reshape(bf16[64,2,768]{2,1,0:T(2,128)(2,1)} %get-tuple-element.6) | data formatting | bytes 393216 | tf_op jit(solution)/shard_map/reshape | solution.py:459
  70.7 0.2 copy.13
  70.9 0.8 %reshape.17 = bf16[2,64,768]{2,1,0:T(8,128)(2,1)} reshape(bf16[2,64,2,384]{3,2,1,0:T(2,128)(2,1)S(1)} %copy.13) | data formatting | bytes 393216 | tf_op jit(solution)/shard_map/reshape | solution.py:460
  71.7 1.5 %copy.16 = f32[2,4,16,128]{3,2,1,0:T(8,128)} copy(f32[2,4,16,128]{3,2,1,0:T(8,128)} %get-tuple-element.13) | data formatting | bytes 131072
  73.2 1.2 %copy.17 = f32[4,128]{1,0:T(4,128)} copy(f32[4,128]{1,0:T(4,128)} %get-tuple-element.14) | data formatting | bytes 4096

commit v4 on v3

--- a/solution.py
+++ b/solution.py
@@ -384,6 +384,15 @@
     wait_bytes(send2.at[pl.ds(0, rows - 1)], send_sem.at[6])
     wait_bytes(gath.at[pl.ds(0, half - 1)], send_sem.at[2])
     wait_bytes(gath.at[pl.ds(0, half - 1)], send_sem.at[3])
+
+
+def arrange(spec_in, ocean_in, heat_in, spec_out, ocean_out, heat_out):
+    mid = spec_in.shape[2] // 2
+    for h in range(2):
+        for u in range(2):
+            spec_out[h, :, u * mid : (u + 1) * mid] = spec_in[:, u, h * mid : (h + 1) * mid]
+    ocean_out[...] = ocean_in[...]
+    heat_out[...] = heat_in[...]
 
 
 def body(
@@ -456,9 +465,16 @@
         remap_weight.reshape(blocks, cells, cells),
         remap_source[:, 0, :].T,
     )
-    spectral = spectral.reshape(waves, 2, hemis, wide // 2)
-    spectral = jnp.transpose(spectral, (2, 0, 1, 3)).reshape(fourier.shape)
-    return spectral, ocean, heat
+    return pl.pallas_call(
+        arrange,
+        out_shape=(
+            jax.ShapeDtypeStruct(fourier.shape, BF),
+            jax.ShapeDtypeStruct(ocean.shape, F32),
+            jax.ShapeDtypeStruct(heat.shape, F32),
+        ),
+        in_specs=[vm, vm, vm],
+        out_specs=(vm, vm, vm),
+    )(spectral, ocean, heat)
 
 
 def solution(mesh):

time: 74.7 us -> 72 us (0.964)
  local copies, waits for them, and re-layouts: 4.73 us -> 0 us
  Pallas kernels: 69 us -> 71.1 us
    unnamed x2 -> x0, local copies, waits for them, and re-layouts: 2.72 us -> none
    pallas_call x0 -> x1, Pallas kernels: none -> 2.11 us  [body(): pl.pallas_call(arrange, out_shape=(jax.ShapeDtypeStruct(fourier.shape, BF...]
    reshape x2 -> x0, local copies, waits for them, and re-layouts: 1.86 us -> none  [the longest x1 1.05 us: body(): spectral = spectral.reshape(waves, 2, hemis, wide // 2)]
where the time goes in v4:
time: 72 us; the launch traced here: 71.8 us
  Pallas kernels  71.1 us (99%)
    pallas_call x1, Pallas kernels, body(): pl.pallas_call(kernel, out_shape=(jax.ShapeDtypeStruct((waves, 2, wide),...  69 us
    pallas_call x1, Pallas kernels, body(): pl.pallas_call(arrange, out_shape=(jax.ShapeDtypeStruct(fourier.shape, BF...  2.11 us

profile of v4, /device:TPU:1, one launch (start us, length us, event | category | flops | bytes accessed | tf_op | source)
XLA Modules:
  0.0 71.8 jit_solution(14379330429866468506)
XLA Ops:
  0.6 69.0 %shard_map.121 = (bf16[64,2,768]{2,1,0:T(2,128)(2,1)}, f32[2,4,16,128]{3,2,1,0:T(8,128)}, f32[4,128]{1,0:T(4,128)}) custom-call(bf16[2,64,768]{2,1,0:T(8,128)(2,1)} %four_hbm.1, bf16[1024,1024]{1,0:T(8,128)(2,1)} %bitcast.5, f32[1024]{0:T(1024)} %gauss_hbm.1, bf16[48]{0:T(256)(128)(2,1)} %kappa_hbm.1, f32[2,4,16,128]{3,2,1,0:T(8,128)} %fields_hbm.1, ...), custom_call_target="tpu_custom_call" | custom-call | tf_op jit(solution)/shard_map/pallas_call | solution.py:418
  69.7 2.1 %shard_map.122 = (bf16[2,64,768]{2,1,0:T(8,128)(2,1)}, f32[2,4,16,128]{3,2,1,0:T(8,128)}, f32[4,128]{1,0:T(4,128)}) custom-call(bf16[64,2,768]{2,1,0:T(2,128)(2,1)} %get-tuple-element.6.spec_in, f32[2,4,16,128]{3,2,1,0:T(8,128)} %get-tuple-element.7.ocean_in, f32[4,128]{1,0:T(4,128)} %get-tuple-element.8.heat_in), custom_call_target="tpu_custom_call" | custom-call | tf_op jit(solution)/shard_map/pallas_call | solution.py:468
